TPU v7x, 32 devices: a whole 2x2x4 slice. The times are simulated.
32 devices in a mesh: row: 4 (over y, x), col: 8 (over z, core).
Axes of the slice: x: 2, y: 2, z: 4, core: 2. Of those that a mesh axis runs over, the one named last changes fastest.
Arguments:
- tiles: bfloat16 [256, 256, 256], P(('row', 'col')), may hold values from -0.09375 to 0.09375
- tile_rows: int32 [256], P(('row', 'col')), may hold values from 0 to 3, as said below
- tile_cols: int32 [256], P(('row', 'col')), may hold values from 0 to 1
- tile_count: int32 [32], P(('row', 'col')), may hold values from 0 to 8, as said below
- bounds: float32 [2], replicated, may hold values from -1 to 2, as said below
- vectors: float32 [4096, 128], P(('row', 'col')), may hold values from -6 to 6
Outputs:
- filtered: float32 [4096, 128], P(('row', 'col'))
- gram: float32 [128, 128], replicated
Inputs may be any that keep to these rules, and one draw needn't show every extreme that they name: `tile_rows`: within each device the first tile_count slots name distinct blocks with global block row I <= global block column J; the device's diagonal blocks (I = J) come first; every diagonal block of the Hamiltonian is stored; slots after the live ones hold valid indices but are not part of the matrix. `tile_count`: devices whose block rows all lie below their block columns have no live slot; some device has all 8 slots live. bounds[0] < -0.5 and bounds[1] > 1.0.
All inputs are finite; a program needn't handle non-finite values.
Results may differ from a plain program's by a relative error of at most 0.0037.
Values may be sent and summed in bfloat16 or wider, within the bound.
A program may use at most 64 MiB of HBM per device.

v0:
```python
import jax
import jax.numpy as jnp
from jax import lax
from jax.sharding import PartitionSpec as P

BLK_COL = 2


def spread(block, axis, holder):
    block = jnp.where(lax.axis_index(axis) == holder, block, jnp.zeros_like(block))
    return lax.psum(block, axis)


def on_device(tiles, tile_rows, tile_cols, tile_count, bounds, vectors):
    col_ratio = lax.axis_size("col") // lax.axis_size("row")
    col_index = lax.axis_index("col")
    row_index = lax.axis_index("row")
    root_row = col_index // col_ratio
    slot_total = tiles.shape[0]
    block_size = tiles.shape[1]
    share_rows = vectors.shape[0]
    width_vecs = vectors.shape[1]
    group_rows = share_rows * lax.axis_size("col")
    group_blocks = group_rows // block_size
    column_rows = BLK_COL * block_size
    total_rows = share_rows * lax.axis_size("row") * lax.axis_size("col")
    offset = col_index % col_ratio * column_rows
    live_mask = (jnp.arange(slot_total, dtype=jnp.int32) < tile_count[0]).astype(jnp.bfloat16)
    owner_flag = (row_index == root_row).astype(jnp.float32)
    center = (bounds[1] + bounds[0]) * 0.5
    halfwidth = (bounds[1] - bounds[0]) * 0.5

    def apply_hamiltonian(current_vec):
        vector_panel = current_vec.astype(jnp.bfloat16)
        row_panel = lax.all_gather(vector_panel, "col", axis=0, tiled=True)
        col_piece = lax.dynamic_slice_in_dim(row_panel, offset, column_rows, 0)
        col_panel = spread(col_piece, "row", root_row)
        row_input = row_panel.reshape(group_blocks, block_size, width_vecs)
        col_input = col_panel.reshape(BLK_COL, block_size, width_vecs)
        start_rows = jnp.zeros((group_blocks, block_size, width_vecs), jnp.float32)
        start_cols = jnp.zeros((BLK_COL, block_size, width_vecs), jnp.float32)
        masked_cols = col_input[tile_cols] * live_mask[:, None, None]
        masked_rows = row_input[tile_rows] * live_mask[:, None, None]
        forward = jnp.einsum("tab,tbk->tak", tiles, masked_cols, preferred_element_type=jnp.float32)
        backward = jnp.einsum(
            "tab,tak->tbk", tiles, masked_rows, preferred_element_type=jnp.float32
        )
        row_part = start_rows.at[tile_rows].add(forward)
        col_part = start_cols.at[tile_cols].add(backward)
        column_total = lax.psum(col_part, "row")
        row_part = row_part.reshape(group_rows, width_vecs)
        present = lax.dynamic_slice_in_dim(row_part, offset, column_rows, 0)
        updated = present + owner_flag * column_total.reshape(column_rows, width_vecs)
        row_part = lax.dynamic_update_slice_in_dim(row_part, updated, offset, 0)
        return lax.psum_scatter(row_part, "col", scatter_dimension=0, tiled=True)

    current_vec = (apply_hamiltonian(vectors) - center * vectors) / halfwidth
    image = apply_hamiltonian(current_vec)
    following = 2.0 * (image - center * current_vec) / halfwidth - vectors
    current_vec = following
    gram_local = lax.dot_general(
        current_vec,
        current_vec,
        (((0,), (0,)), ((), ())),
        precision=lax.Precision.HIGHEST,
        preferred_element_type=jnp.float32,
    )
    gram_total = lax.psum(gram_local, ("row", "col"))
    return (current_vec, gram_total / total_rows)


def solution(mesh):
    in_specs = (
        P(("row", "col"), None, None),
        P(("row", "col")),
        P(("row", "col")),
        P(("row", "col")),
        P(),
        P(("row", "col"), None),
    )
    out_specs = (P(("row", "col"), None), P())
    return jax.shard_map(
        on_device, mesh=mesh, in_specs=in_specs, out_specs=out_specs, check_vma=False
    )
```

profile of v0, /device:TPU:1, one launch (start us, length us, event | category | flops | bytes accessed | tf_op | source)
XLA Modules:
  0.0 414.4 jit_solution(1064199134010569408)
XLA Ops:
  7.2 0.9 convert_element_type.16
  8.2 15.8 %all_gather.6 = bf16[1024,128]{1,0:T(8,128)(2,1)S(1)} all-gather(bf16[128,128]{1,0:T(8,128)(2,1)S(1)} %convert_element_type.16), channel_id=1, replica_groups=mesh['row'=4,'col'=8] {'col'}, dimensions={0}, use_global_device_ids=true | all-gather | bytes 294912 | tf_op jit(solution)/shard_map/all_gather | solution.py:35
  23.9 0.7 dynamic-slice_select_fusion.1
  24.6 0.0 all-reduce.8.cloned.1.call-start
  25.4 0.6 copy-done.9
  26.0 0.6 gather_fusion.1
  26.7 0.4 convolution_bitcast_fusion.2
  27.1 0.3 copy.15
  27.4 0.3 copy-done.10
  27.8 1.3 scatter_fusion.1
  29.1 0.7 copy-done.4
  29.8 0.0 reduce-scatter.3.cloned.1.call-start
  29.9 37.0 %all-reduce.6.cloned.1.call-done = bf16[2,256,128]{2,1,0:T(8,128)(2,1)} async-done(((bf16[2,256,128]{2,1,0:T(8,128)(2,1)}), bf16[2,256,128]{2,1,0:T(8,128)(2,1)}) %all-reduce.6.cloned.1.call-update) | async-done | bytes 131088 | tf_op jit(solution)/shard_map/psum | solution.py:11
  66.9 1.5 gather_fusion
  68.5 1.7 convolution_bitcast_fusion.3
  70.2 1.5 copy.13
  71.8 1.3 scatter_fusion
  73.1 39.9 %all-reduce.8.cloned.1.call-done = f32[2,256,128]{2,1,0:T(8,128)} async-done(((f32[2,256,128]{2,1,0:T(8,128)}), f32[2,256,128]{2,1,0:T(8,128)}) %all-reduce.8.cloned.1.call-update) | async-done | bytes 262160 | tf_op jit(solution)/shard_map/psum | solution.py:50
  113.1 1.0 broadcast_multiply_fusion.1
  114.0 0.1 constant_dynamic-update-slice_fusion.1
  114.1 0.8 copy-done.2
  114.9 0.0 all-reduce.10.cloned.1.call-start
  114.9 0.6 fusion.9
  118.1 25.2 %reduce-scatter.3.cloned.1.call-done = f32[128,128]{1,0:T(8,128)} async-done(((f32[1024,128]{1,0:T(8,128)}), f32[128,128]{1,0:T(8,128)}) %reduce-scatter.3.cloned.1.call-update) | async-done | bytes 65552 | tf_op jit(solution)/shard_map/reduce_scatter | solution.py:55
  143.4 0.9 fusion.8
  144.2 18.0 %all_gather.7 = bf16[1024,128]{1,0:T(8,128)(2,1)S(1)} all-gather(bf16[128,128]{1,0:T(8,128)(2,1)S(1)} %fusion.8), channel_id=1, replica_groups=mesh['row'=4,'col'=8] {'col'}, dimensions={0}, use_global_device_ids=true | all-gather | bytes 294912 | tf_op jit(solution)/shard_map/all_gather | solution.py:35
  162.3 0.7 dynamic-slice_select_fusion
  162.9 0.6 gather_fusion.3
  163.6 0.0 all-reduce.12.cloned.1.call-start
  163.7 0.4 convolution_bitcast_fusion
  164.1 0.3 copy.19
  164.4 1.3 scatter_fusion.3
  165.8 0.7 copy-done.3
  166.5 0.0 reduce-scatter.5.cloned.1.call-start
  166.6 36.5 %all-reduce.10.cloned.1.call-done = bf16[2,256,128]{2,1,0:T(8,128)(2,1)} async-done(((bf16[2,256,128]{2,1,0:T(8,128)(2,1)}), bf16[2,256,128]{2,1,0:T(8,128)(2,1)}) %all-reduce.10.cloned.1.call-update) | async-done | bytes 131088 | tf_op jit(solution)/shard_map/psum | solution.py:11
  203.1 1.5 gather_fusion.2
  204.7 1.7 convolution_bitcast_fusion.1
  206.4 1.5 copy.17
  208.0 1.3 scatter_fusion.2
  209.3 39.5 %all-reduce.12.cloned.1.call-done = f32[2,256,128]{2,1,0:T(8,128)} async-done(((f32[2,256,128]{2,1,0:T(8,128)}), f32[2,256,128]{2,1,0:T(8,128)}) %all-reduce.12.cloned.1.call-update) | async-done | bytes 262160 | tf_op jit(solution)/shard_map/psum | solution.py:50
  248.8 1.0 broadcast_multiply_fusion
  249.8 0.1 constant_dynamic-update-slice_fusion
  249.9 0.8 copy-done.1
  250.7 28.2 %reduce-scatter.5.cloned.1.call-done = f32[128,128]{1,0:T(8,128)} async-done(((f32[1024,128]{1,0:T(8,128)}), f32[128,128]{1,0:T(8,128)}) %reduce-scatter.5.cloned.1.call-update) | async-done | bytes 65552 | tf_op jit(solution)/shard_map/reduce_scatter | solution.py:55
  278.9 0.9 divide_subtract_fusion
  279.8 0.9 fusion.10
  280.8 125.3 %all-reduce.14.cloned.1.call-done = f32[128,128]{1,0:T(8,128)} async-done(((f32[128,128]{1,0:T(8,128)}), f32[128,128]{1,0:T(8,128)}) %all-reduce.14.cloned.1.call-update) | async-done | bytes 65552 | tf_op jit(solution)/shard_map/psum | solution.py:68
  406.1 1.5 broadcast_multiply_fusion.2
  (34 shorter events, 0.4 us)
Async XLA Ops:
  7.2 19.5 %copy-start = (bf16[8,256,256]{2,1,0:T(8,128)(2,1)S(1)}, bf16[8,256,256]{2,1,0:T(8,128)(2,1)}, u32[]{:S(2)}) copy-start(bf16[8,256,256]{2,1,0:T(8,128)(2,1)} %param.6) | copy-start | bytes 3145732
  7.2 59.8 %all-reduce.6.cloned.1.call-start = ((), (), s32[]{:S(2)}) async-start(), calls=%async_computation.2 | async-start | bytes 262144 | tf_op jit(solution)/shard_map/psum | solution.py:11
  24.6 88.4 %all-reduce.8.cloned.1.call-start = ((), (), s32[]{:S(2)}) async-start(), calls=%async_computation.3 | async-start | bytes 524288 | tf_op jit(solution)/shard_map/psum | solution.py:50
  25.3 0.7 copy-start.9
  27.1 0.7 copy-start.10
  29.1 0.7 copy-start.4
  29.8 113.5 %reduce-scatter.3.cloned.1.call-start = ((), (), s32[]{:S(2)}) async-start(), calls=%async_computation.4 | async-start | bytes 589824 | tf_op jit(solution)/shard_map/reduce_scatter | solution.py:55
  114.1 0.8 copy-start.2
  114.1 0.9 copy-start.8
  114.1 29.3 %copy-start.5 = (f32[128,128]{1,0:T(8,128)S(1)}, f32[128,128]{1,0:T(8,128)}, u32[]{:S(2)}) copy-start(f32[128,128]{1,0:T(8,128)} %param.11) | copy-start | bytes 196612
  114.9 88.2 %all-reduce.10.cloned.1.call-start = ((), (), s32[]{:S(2)}) async-start(), calls=%async_computation.5 | async-start | bytes 262144 | tf_op jit(solution)/shard_map/psum | solution.py:11
  163.6 85.2 %all-reduce.12.cloned.1.call-start = ((), (), s32[]{:S(2)}) async-start(), calls=%async_computation.6 | async-start | bytes 524288 | tf_op jit(solution)/shard_map/psum | solution.py:50
  165.8 0.7 copy-start.3
  166.5 112.4 %reduce-scatter.5.cloned.1.call-start = ((), (), s32[]{:S(2)}) async-start(), calls=%async_computation.7 | async-start | bytes 589824 | tf_op jit(solution)/shard_map/reduce_scatter | solution.py:55
  249.9 0.8 copy-start.1
  249.9 29.1 %copy-start.7 = (f32[128,128]{1,0:T(8,128)S(1)}, f32[128,128]{1,0:T(8,128)}, u32[]{:S(2)}) copy-start(f32[128,128]{1,0:T(8,128)} %reduce-scatter.3.cloned.1.call-done) | copy-start | bytes 196612
  250.7 155.4 %all-reduce.14.cloned.1.call-start = ((), (), s32[]{:S(2)}) async-start(), calls=%async_computation.8 | async-start | bytes 131072 | tf_op jit(solution)/shard_map/psum | solution.py:68
  279.8 0.9 copy-start.6
Sparse Core Ops, SparseCore 0:
  24.8 42.1 all-reduce.5
  70.1 42.8 all-reduce.7
  115.3 28.0 reduce-scatter.2
  163.7 39.3 all-reduce.9
  205.9 42.9 all-reduce.11
  251.0 27.8 reduce-scatter.4
  285.1 120.9 all-reduce.13
where the time goes:
time: 415 us; the launch traced here: 414 us
  waiting for transfers between devices  332 us (80%)
  blocking collectives  33.8 us (8%)
  between operations  17.7 us (4%)
  local copies, waits for them, and re-layouts  12.8 us (3%)
  other arithmetic  12.8 us (3%)
  matrix products  5.15 us (1%)
    psum x1, waiting for transfers between devices, on_device(): gram_total = lax.psum(gram_local, ('row', 'col'))  125 us
    psum x2, waiting for transfers between devices, apply_hamiltonian(): column_total = lax.psum(col_part, 'row')  79.5 us
    psum x2, waiting for transfers between devices, spread(): return lax.psum(block, axis)  73.6 us
    reduce_scatter x2, waiting for transfers between devices, apply_hamiltonian(): return lax.psum_scatter(row_part, 'col', scatter_dimension=0, tiled=True)  53.5 us
    all_gather x2, blocking collectives, apply_hamiltonian(): row_panel = lax.all_gather(vector_panel, 'col', axis=0, tiled=True)  33.8 us
  transfers between devices with their start and end apart: 7, of which 7 were waited for; matrix products, arithmetic and copies ran while one was open for 4% of the time, Pallas kernels for 0%

commit v1 on v0

--- a/solution.py
+++ b/solution.py
@@ -8,7 +8,7 @@
 
 def spread(block, axis, holder):
     block = jnp.where(lax.axis_index(axis) == holder, block, jnp.zeros_like(block))
-    return lax.psum(block, axis)
+    return jnp.sum(lax.all_gather(block, axis), axis=0)
 
 
 def on_device(tiles, tile_rows, tile_cols, tile_count, bounds, vectors):

time: 415 us -> 343 us (0.83)
  waiting for transfers between devices: 332 us -> 243 us
  blocking collectives: 33.8 us -> 54.1 us
    psum x2 -> x0, waiting for transfers between devices: 73.6 us -> none  [spread(): return lax.psum(block, axis)]
    all_gather x0 -> x2, blocking collectives: none -> 20 us  [spread(): return jnp.sum(lax.all_gather(block, axis), axis=0)]
    psum x2, waiting for transfers between devices: 79.5 us -> 64 us  [apply_hamiltonian(): column_total = lax.psum(col_part, 'row')]
  transfers between devices with their start and end apart: 7 -> 5, of which waited for: 7 -> 5; matrix products, arithmetic and copies ran while one was open for 4% -> 3% of each run, Pallas kernels for 0% -> 0%
where the time goes in v1:
time: 343 us
  waiting for transfers between devices  243 us (71%)
  blocking collectives  54.1 us (16%)
  between operations  17.4 us (5%)
  other arithmetic  11.7 us (3%)
  local copies, waits for them, and re-layouts  11.6 us (3%)
  matrix products  5.16 us (2%)
    psum x1, waiting for transfers between devices, on_device(): gram_total = lax.psum(gram_local, ('row', 'col'))  125 us
    psum x2, waiting for transfers between devices, apply_hamiltonian(): column_total = lax.psum(col_part, 'row')  64 us
    reduce_scatter x2, waiting for transfers between devices, apply_hamiltonian(): return lax.psum_scatter(row_part, 'col', scatter_dimension=0, tiled=True)  53.4 us
    all_gather x2, blocking collectives, apply_hamiltonian(): row_panel = lax.all_gather(vector_panel, 'col', axis=0, tiled=True)  34.1 us
    all_gather x2, blocking collectives, spread(): return jnp.sum(lax.all_gather(block, axis), axis=0)  20 us
  transfers between devices with their start and end apart: 5, of which 5 were waited for; matrix products, arithmetic and copies ran while one was open for 3% of the time, Pallas kernels for 0%

profile of v1, /device:TPU:1, one launch (start us, length us, event | category | flops | bytes accessed | tf_op | source)
XLA Modules:
  0.0 342.7 jit_solution(13657085534069359991)
XLA Ops:
  7.2 0.0 all-reduce.4.cloned.1.call-start
  7.2 0.9 convert_element_type.20
  8.2 15.9 %all_gather.18 = bf16[1024,128]{1,0:T(8,128)(2,1)S(1)} all-gather(bf16[128,128]{1,0:T(8,128)(2,1)S(1)} %convert_element_type.20), channel_id=1, replica_groups=mesh['row'=4,'col'=8] {'col'}, dimensions={0}, use_global_device_ids=true | all-gather | bytes 294912 | tf_op jit(solution)/shard_map/all_gather | solution.py:35
  24.7 0.6 copy-done.13
  25.4 0.6 gather_fusion.1
  26.1 0.4 convolution_bitcast_fusion.2
  26.5 0.3 copy.15
  26.8 1.3 scatter_fusion.1
  28.2 0.7 copy-done.4
  28.9 0.0 reduce-scatter.3.cloned.1.call-start
  29.0 0.2 copy-done.6
  29.2 11.0 %all-gather = bf16[2048,128]{1,0:T(8,128)(2,1)S(1)} all-gather(bf16[512,128]{1,0:T(8,128)(2,1)S(1)} %dynamic-slice_select_fusion.1), channel_id=2, replica_groups=mesh['row'=4,'col'=8] {'row'}, dimensions={0}, use_global_device_ids=true | all-gather | bytes 655360 | tf_op jit(solution)/shard_map/all_gather | solution.py:11
  40.2 0.1 reduce_sum.24
  40.3 0.6 gather_fusion
  41.0 1.7 convolution_bitcast_fusion.3
  42.7 1.5 copy.13
  44.3 1.3 scatter_fusion
  45.6 27.9 %all-reduce.4.cloned.1.call-done = f32[2,256,128]{2,1,0:T(8,128)} async-done(((f32[2,256,128]{2,1,0:T(8,128)}), f32[2,256,128]{2,1,0:T(8,128)}) %all-reduce.4.cloned.1.call-update) | async-done | bytes 262160 | tf_op jit(solution)/shard_map/psum | solution.py:50
  73.5 1.0 broadcast_multiply_fusion.1
  74.4 0.1 constant_dynamic-update-slice_fusion.1
  74.5 0.8 copy-done.2
  75.3 0.0 all-reduce.6.cloned.1.call-start
  75.4 0.6 fusion.9
  78.5 25.2 %reduce-scatter.3.cloned.1.call-done = f32[128,128]{1,0:T(8,128)} async-done(((f32[1024,128]{1,0:T(8,128)}), f32[128,128]{1,0:T(8,128)}) %reduce-scatter.3.cloned.1.call-update) | async-done | bytes 65552 | tf_op jit(solution)/shard_map/reduce_scatter | solution.py:55
  103.7 0.9 fusion.8
  104.6 18.2 %all_gather.21 = bf16[1024,128]{1,0:T(8,128)(2,1)S(1)} all-gather(bf16[128,128]{1,0:T(8,128)(2,1)S(1)} %fusion.8), channel_id=1, replica_groups=mesh['row'=4,'col'=8] {'col'}, dimensions={0}, use_global_device_ids=true | all-gather | bytes 294912 | tf_op jit(solution)/shard_map/all_gather | solution.py:35
  122.8 9.0 %all-gather.1 = bf16[2048,128]{1,0:T(8,128)(2,1)S(1)} all-gather(bf16[512,128]{1,0:T(8,128)(2,1)S(1)} %dynamic-slice_select_fusion), channel_id=3, replica_groups=mesh['row'=4,'col'=8] {'row'}, dimensions={0}, use_global_device_ids=true | all-gather | bytes 655360 | tf_op jit(solution)/shard_map/all_gather | solution.py:11
  131.8 0.1 reduce_sum.25
  131.9 1.4 gather_fusion.2
  133.3 0.6 gather_fusion.3
  133.9 0.4 convolution_bitcast_fusion
  134.3 0.3 copy.19
  134.7 1.3 scatter_fusion.3
  136.0 0.7 copy-done.3
  136.8 0.0 reduce-scatter.5.cloned.1.call-start
  136.8 1.7 convolution_bitcast_fusion.1
  138.5 1.5 copy.17
  140.1 1.3 scatter_fusion.2
  141.5 36.1 %all-reduce.6.cloned.1.call-done = f32[2,256,128]{2,1,0:T(8,128)} async-done(((f32[2,256,128]{2,1,0:T(8,128)}), f32[2,256,128]{2,1,0:T(8,128)}) %all-reduce.6.cloned.1.call-update) | async-done | bytes 262160 | tf_op jit(solution)/shard_map/psum | solution.py:50
  177.6 1.0 broadcast_multiply_fusion
  178.6 0.1 constant_dynamic-update-slice_fusion
  178.7 0.8 copy-done.1
  179.4 0.0 all-reduce.8.cloned.1.call-start
  179.5 28.2 %reduce-scatter.5.cloned.1.call-done = f32[128,128]{1,0:T(8,128)} async-done(((f32[1024,128]{1,0:T(8,128)}), f32[128,128]{1,0:T(8,128)}) %reduce-scatter.5.cloned.1.call-update) | async-done | bytes 65552 | tf_op jit(solution)/shard_map/reduce_scatter | solution.py:55
  207.7 0.9 divide_subtract_fusion
  208.6 0.9 fusion.10
  209.5 125.1 %all-reduce.8.cloned.1.call-done = f32[128,128]{1,0:T(8,128)} async-done(((f32[128,128]{1,0:T(8,128)}), f32[128,128]{1,0:T(8,128)}) %all-reduce.8.cloned.1.call-update) | async-done | bytes 65552 | tf_op jit(solution)/shard_map/psum | solution.py:68
  334.7 1.5 broadcast_multiply_fusion.2
  (38 shorter events, 0.3 us)
Async XLA Ops:
  7.2 18.9 %copy-start = (bf16[8,256,256]{2,1,0:T(8,128)(2,1)S(1)}, bf16[8,256,256]{2,1,0:T(8,128)(2,1)}, u32[]{:S(2)}) copy-start(bf16[8,256,256]{2,1,0:T(8,128)(2,1)} %param.6) | copy-start | bytes 3145732
  7.2 66.3 %all-reduce.4.cloned.1.call-start = ((), (), s32[]{:S(2)}) async-start(), calls=%async_computation.2 | async-start | bytes 524288 | tf_op jit(solution)/shard_map/psum | solution.py:50
  8.1 15.9 %copy-start.12 = (s32[8]{0:T(128)S(1)}, s32[8]{0:T(128)}, u32[]{:S(2)}) copy-start(s32[8]{0:T(128)} %param.8) | copy-start | bytes 100
  24.0 2.0 copy-start.5
  24.7 0.7 copy-start.13
  28.1 0.7 copy-start.4
  28.2 1.0 copy-start.6
  28.9 74.8 %reduce-scatter.3.cloned.1.call-start = ((), (), s32[]{:S(2)}) async-start(), calls=%async_computation.3 | async-start | bytes 589824 | tf_op jit(solution)/shard_map/reduce_scatter | solution.py:55
  74.5 0.8 copy-start.2
  74.5 0.9 copy-start.11
  74.5 29.2 %copy-start.8 = (f32[128,128]{1,0:T(8,128)S(1)}, f32[128,128]{1,0:T(8,128)}, u32[]{:S(2)}) copy-start(f32[128,128]{1,0:T(8,128)} %param.11) | copy-start | bytes 196612
  75.3 102.3 %all-reduce.6.cloned.1.call-start = ((), (), s32[]{:S(2)}) async-start(), calls=%async_computation.4 | async-start | bytes 524288 | tf_op jit(solution)/shard_map/psum | solution.py:50
  134.7 2.1 copy-start.7
  136.0 0.7 copy-start.3
  136.8 70.9 %reduce-scatter.5.cloned.1.call-start = ((), (), s32[]{:S(2)}) async-start(), calls=%async_computation.5 | async-start | bytes 589824 | tf_op jit(solution)/shard_map/reduce_scatter | solution.py:55
  178.6 0.8 copy-start.1
  178.6 29.1 %copy-start.10 = (f32[128,128]{1,0:T(8,128)S(1)}, f32[128,128]{1,0:T(8,128)}, u32[]{:S(2)}) copy-start(f32[128,128]{1,0:T(8,128)} %reduce-scatter.3.cloned.1.call-done) | copy-start | bytes 196612
  179.4 155.2 %all-reduce.8.cloned.1.call-start = ((), (), s32[]{:S(2)}) async-start(), calls=%async_computation.6 | async-start | bytes 131072 | tf_op jit(solution)/shard_map/psum | solution.py:68
  208.6 0.9 copy-start.9
Sparse Core Ops, SparseCore 0:
  29.0 44.4 all-reduce.3
  75.8 27.8 reduce-scatter.2
  136.9 40.6 all-reduce.5
  179.8 27.8 reduce-scatter.4
  213.7 120.9 all-reduce.7
